TPU v7x, 32 devices: a whole 2x2x4 slice. The times are simulated.
32 devices in a mesh: lon: 8 (over z, x), lat: 4 (over y, core).
Axes of the slice: x: 2, y: 2, z: 4, core: 2. Of those that a mesh axis runs over, the one named last changes fastest.
Arguments:
- sounding_kernel: float32 [72, 32768], P(None, ('lon', 'lat')), may hold values from 0.2 to 1.4
- sounding_misfit: float32 [32768], P(('lon', 'lat')), may hold values from -6 to 6
- sounding_owner: int32 [32768, 1], P(('lon', 'lat')), may hold values from 0 to 31; in each aligned block of 1024 rows (0 to 1023, 1024 to 2047, ...) at most 48 rows name the same one
- sounding_cell: int32 [32768], P(('lon', 'lat')), may hold values from 0 to 1023
- sounding_step: int32 [32768], P(('lon', 'lat')), may hold values from 0 to 1
- sounding_count: int32 [32], P(('lon', 'lat')), may hold values from 512 to 1024, as said below
- courant_x: float32 [72, 32, 1024], P(None, 'lat', 'lon'), may hold values from -0.45 to 0.45
- courant_y: float32 [72, 32, 1024], P(None, 'lat', 'lon'), may hold values from -0.45 to 0.45
- diffusivity: float32 [72, 32, 1024], P(None, 'lat', 'lon'), may hold values from 0.05 to 3000
- region_map: int32 [32, 1024], P('lat', 'lon'), may hold values from 0 to 4095, as said below
- region_owner: int32 [4096], replicated, may hold values from 0 to 4095, as said below
Outputs:
- adjoint_field: float32 [72, 32, 1024], P(None, 'lat', 'lon')
- region_sensitivity: float32 [2, 4096], P(None, ('lon', 'lat'))
Inputs may be any that keep to these rules, and one draw needn't show every extreme that they name: `sounding_owner`: at most 48 soundings of one device name one owner, and some device sends exactly 48 to some owner. Only the first sounding_count slots of a device hold real soundings; some device has all 1024. `region_map`: of one device's columns, at most 64 lie in regions whose positions share one owner, and every device has exactly 64 columns for some owner. `region_owner`: each position is taken by exactly one region.
All inputs are finite; a program needn't handle non-finite values.
Results may differ from a plain program's by a relative error of at most 0.0003.
Values sent between devices are 32-bit elements; how exact they have to be, the bound alone decides.
A program may use at most 128 MiB of HBM per device.

v0:
```python
import jax
import jax.numpy as jnp
from jax import lax
from jax.sharding import PartitionSpec as P

STEPS = 2


def with_halo(x, sides, width):
    for axis, dim in sides:
        size, length = (lax.axis_size(axis), x.shape[dim])
        up = [(i, (i + 1) % size) for i in range(size)]
        down = [(j, i) for i, j in up]
        last = lax.slice_in_dim(x, length - width, length, axis=dim)
        leading = lax.slice_in_dim(x, 0, width, axis=dim)
        before = lax.ppermute(last, axis, up)
        after = lax.ppermute(leading, axis, down)
        x = jnp.concatenate([before, x, after], axis=dim)
    return x


def advect(padded, courant_x, courant_y):
    center = padded[:, 1:-1, 1:-1]
    west = padded[:, 1:-1, :-2]
    east = padded[:, 1:-1, 2:]
    south = padded[:, :-2, 1:-1]
    north = padded[:, 2:, 1:-1]
    return (
        center
        - jnp.maximum(courant_x, 0.0) * (center - west)
        - jnp.maximum(-courant_x, 0.0) * (center - east)
        - jnp.maximum(courant_y, 0.0) * (center - south)
        - jnp.maximum(-courant_y, 0.0) * (center - north)
    )


def diffuse(field, coupling):
    below = jnp.concatenate([jnp.zeros_like(coupling[:1]), coupling[:-1]], axis=0)
    middle = 1.0 + below + coupling

    def forward(carry, item):
        w_prev, g_prev = carry
        low, mid, upper, rhs = item
        denom = mid + low * w_prev
        w_now = -upper / denom
        g_now = (rhs + low * g_prev) / denom
        return ((w_now, g_now), (w_now, g_now))

    zero = jnp.zeros_like(field[0])
    _, (w_all, g_all) = lax.scan(forward, (zero, zero), (below, middle, coupling, field))

    def backward(x_next, item):
        w_now, g_now = item
        x_now = g_now - w_now * x_next
        return (x_now, x_now)

    _, solved = lax.scan(backward, zero, (w_all, g_all), reverse=True)
    return solved


def lat_mask(rows_lat, width):
    first = lax.axis_index("lat") * rows_lat - width
    inside = first + jnp.arange(rows_lat + 2 * width, dtype=jnp.int32)
    limit = rows_lat * lax.axis_size("lat")
    return ((inside >= 0) & (inside < limit)).astype(jnp.float32)[:, None]


def body(
    sounding_kernel,
    sounding_misfit,
    sounding_owner,
    sounding_cell,
    sounding_step,
    sounding_count,
    courant_x,
    courant_y,
    diffusivity,
    region_map,
    region_owner,
):
    levels, rows_lat, rows_lon = courant_x.shape
    cells = rows_lat * rows_lon
    lon_count = lax.axis_size("lon")
    lat_count = lax.axis_size("lat")
    devices = lon_count * lat_count
    per_device = sounding_misfit.shape[0]
    capacity = max(2, 3 * per_device // (2 * devices))
    regions = region_owner.shape[0]
    slots = jnp.arange(per_device, dtype=jnp.int32)
    valid = slots < sounding_count[0]
    owner = sounding_owner[:, 0]
    earlier = (
        (owner[:, None] == owner[None, :]) & (slots[:, None] < slots[None, :]) & valid[:, None]
    )
    rank = jnp.sum(earlier.astype(jnp.int32), axis=0)
    spill = devices * capacity
    target = jnp.where(valid, owner * capacity + rank, spill)
    forcing = sounding_misfit[:, None] * sounding_kernel.T
    code = (sounding_step * cells + sounding_cell).astype(jnp.float32)
    send_rows = jax.ops.segment_sum(forcing, target, num_segments=spill + 1)[:spill]
    send_code = jax.ops.segment_sum(code, target, num_segments=spill + 1)[:spill]
    send_rows = send_rows.reshape(lon_count, lat_count, capacity * levels)
    send_code = send_code.reshape(lon_count, lat_count, capacity)
    got_rows, got_code = (
        lax.all_to_all(
            lax.all_to_all(send_rows, "lon", split_axis=0, concat_axis=0, tiled=True),
            "lat",
            split_axis=1,
            concat_axis=1,
            tiled=True,
        ),
        lax.all_to_all(
            lax.all_to_all(send_code, "lon", split_axis=0, concat_axis=0, tiled=True),
            "lat",
            split_axis=1,
            concat_axis=1,
            tiled=True,
        ),
    )
    got_rows = got_rows.reshape(devices * capacity, levels)
    got_code = got_code.reshape(-1).astype(jnp.int32)
    deposit = jax.ops.segment_sum(got_rows, got_code, num_segments=STEPS * cells)
    deposit = (
        deposit.reshape(STEPS, cells, levels)
        .transpose(0, 2, 1)
        .reshape(STEPS, levels, rows_lat, rows_lon)
    )
    field = jnp.zeros((levels, rows_lat, rows_lon), jnp.float32)
    surfaces = []
    for step in range(STEPS):
        field = field + deposit[step]
        padded = with_halo(field, (("lon", 2), ("lat", 1)), 1)
        padded = padded * lat_mask(rows_lat, 1)
        field = diffuse(advect(padded, courant_x, courant_y), diffusivity)
        surfaces.append(field[0])
    positions = region_owner[region_map].reshape(-1)

    def region_partial(surface):
        return jax.ops.segment_sum(surface.reshape(-1), positions, num_segments=regions)

    partial_all = jnp.stack([region_partial(surface) for surface in surfaces])
    totals = lax.psum_scatter(partial_all, ("lon", "lat"), scatter_dimension=1, tiled=True)
    return (field, totals)


def solution(mesh):
    placed = (
        P(None, ("lon", "lat")),
        P(("lon", "lat")),
        P(("lon", "lat"), None),
        P(("lon", "lat")),
        P(("lon", "lat")),
        P(("lon", "lat")),
        P(None, "lat", "lon"),
        P(None, "lat", "lon"),
        P(None, "lat", "lon"),
        P("lat", "lon"),
        P(),
    )
    return jax.shard_map(
        body,
        mesh=mesh,
        in_specs=placed,
        out_specs=(P(None, "lat", "lon"), P(None, ("lon", "lat"))),
        check_vma=False,
    )
```

profile of v0, /device:TPU:0, one launch (start us, length us, event | category | flops | bytes accessed | tf_op | source)
XLA Modules:
  0.0 293.2 jit_solution(7118222374705873824)
XLA Ops:
  7.9 2.0 convert_reduce_fusion
  11.2 6.2 %scatter_custom_fusion = f32[1537]{0:T(1024)S(1)} fusion(s32[1024]{0:T(1024)S(1)} %bitcast.137, f32[1024]{0:T(1024)S(1)} %add_convert_fusion, f32[]{:T(128)} %constant.119.clone.1), kind=kCustom, calls=%fused_computation.85 | custom fusion | flops 1024 | bytes 6152 | tf_op jit(solution)/shard_map/scatter-add | solution.py:101
  18.2 7.5 %all-to-all-start = ((f32[8,1,192]{2,1,0:T(1,128)}), f32[8,1,192]{2,1,0:T(1,128)S(1)}, u32[]{:S(2)}, u32[]{:S(2)}) async-start(f32[8,1,192]{2,1,0:T(1,128)} %reshape.125), calls=%async_computation | async-start | bytes 16384 | tf_op jit(solution)/shard_map/all_to_all | solution.py:113
  25.7 1.0 multiply_bitcast_fusion
  26.8 6.3 %scatter_custom_fusion.1 = f32[1537,72]{1,0:T(8,128)S(1)} fusion(s32[1024]{0:T(1024)S(1)} %bitcast.138, f32[1024,72]{1,0:T(8,128)S(1)} %copy.29, f32[]{:T(128)} %constant.119.clone.1), kind=kCustom, calls=%fused_computation.36 | custom fusion | flops 73728 | bytes 442660 | tf_op jit(solution)/shard_map/scatter-add | solution.py:100
  33.2 1.5 reshape.56
  34.7 6.3 %all-to-all-start.2 = ((f32[8,4,3456]{2,1,0:T(4,128)}), f32[8,4,3456]{2,1,0:T(4,128)S(1)}, u32[]{:S(2)}, u32[]{:S(2)}) async-start(f32[8,4,3456]{2,1,0:T(4,128)} %reshape.56), calls=%async_computation.2 | async-start | bytes 884736 | tf_op jit(solution)/shard_map/all_to_all | solution.py:106
  43.0 10.7 %all-to-all-done.2 = f32[8,4,3456]{2,1,0:T(4,128)S(1)} async-done(((f32[8,4,3456]{2,1,0:T(4,128)}), f32[8,4,3456]{2,1,0:T(4,128)S(1)}, u32[]{:S(2)}, u32[]{:S(2)}) %all-to-all-start.2) | async-done | bytes 442400 | tf_op jit(solution)/shard_map/all_to_all | solution.py:106
  53.7 3.2 %all-to-all-start.1 = ((f32[4,1,384]{2,1,0:T(1,128)}), f32[4,1,384]{2,1,0:T(1,128)S(1)}, u32[]{:S(2)}, u32[]{:S(2)}) async-start(f32[4,1,384]{2,1,0:T(1,128)} %reshape.127), calls=%async_computation.1 | async-start | bytes 12288 | tf_op jit(solution)/shard_map/all_to_all | solution.py:112
  57.7 3.0 %all-to-all-done.1 = f32[4,1,384]{2,1,0:T(1,128)S(1)} async-done(((f32[4,1,384]{2,1,0:T(1,128)}), f32[4,1,384]{2,1,0:T(1,128)S(1)}, u32[]{:S(2)}, u32[]{:S(2)}) %all-to-all-start.1) | async-done | bytes 6176 | tf_op jit(solution)/shard_map/all_to_all | solution.py:112
  60.7 3.5 %all-to-all-start.3 = ((f32[8,4,3456]{2,0,1:T(8,128)}), f32[8,4,3456]{2,0,1:T(8,128)S(1)}, u32[]{:S(2)}, u32[]{:S(2)}) async-start(f32[8,4,3456]{2,0,1:T(8,128)} %copy.30), calls=%async_computation.3 | async-start | bytes 884736 | tf_op jit(solution)/shard_map/all_to_all | solution.py:105
  65.1 7.0 %all-to-all-done.3 = f32[8,4,3456]{2,0,1:T(8,128)S(1)} async-done(((f32[8,4,3456]{2,0,1:T(8,128)}), f32[8,4,3456]{2,0,1:T(8,128)S(1)}, u32[]{:S(2)}, u32[]{:S(2)}) %all-to-all-start.3) | async-done | bytes 442400 | tf_op jit(solution)/shard_map/all_to_all | solution.py:105
  73.0 9.8 %scatter_custom_fusion.2 = f32[2048,72]{1,0:T(8,128)S(1)} fusion(s32[1536]{0:T(1024)S(1)} %reshape.85, f32[1536,72]{1,0:T(8,128)S(1)} %reshape.87, f32[]{:T(128)} %constant.119.clone.1), kind=kCustom, calls=%fused_computation.34 | custom fusion | flops 110592 | bytes 589828 | tf_op jit(solution)/shard_map/scatter-add | solution.py:122
  84.7 4.0 %collective-permute-start.1 = (f32[72,8,1]{2,1,0:T(8,128)S(1)}, f32[72,8,1]{2,1,0:T(8,128)S(1)}, u32[]{:S(2)}, u32[]{:S(2)}) collective-permute-start(f32[72,8,1]{2,1,0:T(8,128)S(1)} %get-tuple-element.487), channel_id=1, source_target_pairs={{4,0},{8,4},{12,8},{16,12},{20,16},{24,20},{28,24},{0,28},{5,1},{9... | collective-permute-start | bytes 6920 | tf_op jit(solution)/shard_map/ppermute | solution.py:17
  88.8 9.0 %collective-permute-done = f32[72,8,1]{2,1,0:T(8,128)S(1)} collective-permute-done((f32[72,8,1]{2,1,0:T(8,128)S(1)}, f32[72,8,1]{2,1,0:T(8,128)S(1)}, u32[]{:S(2)}, u32[]{:S(2)}) %collective-permute-start) | collective-permute-done | bytes 2336 | tf_op jit(solution)/shard_map/ppermute | solution.py:16
  97.8 2.2 collective-permute-done.1
  100.6 1.7 collective-permute-start.3
  102.4 2.0 collective-permute-done.2
  105.5 2.8 while.68
  108.3 2.5 while.69
  111.4 4.4 %collective-permute-start.5 = (f32[72,8,1]{2,1,0:T(8,128)S(1)}, f32[72,8,1]{2,1,0:T(8,128)S(1)}, u32[]{:S(2)}, u32[]{:S(2)}) collective-permute-start(f32[72,8,1]{2,1,0:T(8,128)S(1)} %get-tuple-element.485), channel_id=1, source_target_pairs={{4,0},{8,4},{12,8},{16,12},{20,16},{24,20},{28,24},{0,28},{5,1},{9... | collective-permute-start | bytes 6920 | tf_op jit(solution)/shard_map/ppermute | solution.py:17
  115.9 6.2 %gather_fusion = s32[1024]{0:T(1024)S(1)} fusion(s32[4096]{0:T(1024)S(1)} %copy-done, s32[1024]{0:T(1024)S(1)} %fusion.33), kind=kCustom, calls=%fused_computation | custom fusion | bytes 12288 | tf_op jit(solution)/shard_map/gather | solution.py:136
  122.0 2.9 collective-permute-done.4
  124.9 2.4 collective-permute-done.5
  127.9 1.7 collective-permute-start.7
  129.7 5.9 %scatter_custom_fusion.3 = f32[4096]{0:T(1024)S(1)} fusion(s32[1024]{0:T(1024)S(1)} %gather_fusion, f32[1024]{0:T(1024)S(1)} %slice_bitcast_fusion.1, f32[]{:T(128)} %constant.119.clone.1), kind=kCustom, calls=%fused_computation.77 | custom fusion | flops 1024 | bytes 16388 | tf_op jit(solution)/shard_map/scatter-add | solution.py:139
  136.7 3.0 %while.70 = (s32[]{:T(128)}, f32[8,128]{1,0:T(8,128)S(1)}, f32[8,128]{1,0:T(8,128)S(1)}, f32[72,8,128]{2,1,0:T(8,128)S(1)}, f32[72,8,128]{2,1,0:T(8,128)S(1)}, /...) while((s32[]{:T(128)}, f32[8,128]{1,0:T(8,128)S(1)}, ...), condition=%wide.region_9.10_spmd.clone, body=%wide.region_8.9_spmd.clone.sunk | while | flops 9219 | bytes 41083 | solution.py:50
  139.7 2.5 while.71
  142.3 6.1 %scatter_custom_fusion.4 = f32[4096]{0:T(1024)S(1)} fusion(s32[1024]{0:T(1024)} %copy-done.6, f32[1024]{0:T(1024)S(1)} %slice_bitcast_fusion, f32[]{:T(128)} %constant.119.clone.1), kind=kCustom, calls=%fused_computation.75 | custom fusion | flops 1024 | bytes 16896 | tf_op jit(solution)/shard_map/scatter-add | solution.py:139
  148.4 2.0 copy.33
  150.4 134.5 %reduce-scatter.4.cloned.1.call-done = f32[128,2]{1,0:T(8,128)} async-done(((f32[4096,2]{1,0:T(8,128)}), f32[128,2]{1,0:T(8,128)}) %reduce-scatter.4.cloned.1.call-update) | async-done | bytes 1040
  284.9 1.5 copy.34
  (363 shorter events, 16.8 us)
Async XLA Ops:
  7.2 108.7 %copy-start = (s32[4096]{0:T(1024)S(1)}, s32[4096]{0:T(1024)}, u32[]{:S(2)}) copy-start(s32[4096]{0:T(1024)} %param.29) | copy-start | bytes 49156
  18.2 16.5 %all-to-all-start = ((f32[8,1,192]{2,1,0:T(1,128)}), f32[8,1,192]{2,1,0:T(1,128)S(1)}, u32[]{:S(2)}, u32[]{:S(2)}) async-start(f32[8,1,192]{2,1,0:T(1,128)} %reshape.125), calls=%async_computation | async-start | bytes 16384 | tf_op jit(solution)/shard_map/all_to_all | solution.py:113
  34.7 18.9 %all-to-all-start.2 = ((f32[8,4,3456]{2,1,0:T(4,128)}), f32[8,4,3456]{2,1,0:T(4,128)S(1)}, u32[]{:S(2)}, u32[]{:S(2)}) async-start(f32[8,4,3456]{2,1,0:T(4,128)} %reshape.56), calls=%async_computation.2 | async-start | bytes 884736 | tf_op jit(solution)/shard_map/all_to_all | solution.py:106
  53.7 7.0 %all-to-all-start.1 = ((f32[4,1,384]{2,1,0:T(1,128)}), f32[4,1,384]{2,1,0:T(1,128)S(1)}, u32[]{:S(2)}, u32[]{:S(2)}) async-start(f32[4,1,384]{2,1,0:T(1,128)} %reshape.127), calls=%async_computation.1 | async-start | bytes 12288 | tf_op jit(solution)/shard_map/all_to_all | solution.py:112
  60.7 11.4 %all-to-all-start.3 = ((f32[8,4,3456]{2,0,1:T(8,128)}), f32[8,4,3456]{2,0,1:T(8,128)S(1)}, u32[]{:S(2)}, u32[]{:S(2)}) async-start(f32[8,4,3456]{2,0,1:T(8,128)} %copy.30), calls=%async_computation.3 | async-start | bytes 884736 | tf_op jit(solution)/shard_map/all_to_all | solution.py:105
  64.2 220.7 %reduce-scatter.4.cloned.1.call-start = ((), (), s32[]{:S(2)}) async-start(), calls=%async_computation.5 | async-start | bytes 2162688
  83.3 5.4 %copy-start.1 = (f32[72,8,128]{2,1,0:T(8,128)S(1)}, f32[72,8,128]{2,1,0:T(8,128)}, u32[]{:S(2)}) copy-start(f32[72,8,128]{2,1,0:T(8,128)} %param.27) | copy-start | bytes 884740
  83.3 5.4 %slice-start = ((f32[72,8,128]{2,1,0:T(8,128)}), f32[71,8,128]{2,1,0:T(8,128)S(1)}, s32[]{:S(2)}) async-start(f32[72,8,128]{2,1,0:T(8,128)} %param.27), calls=%async_computation.6 | async-start | bytes 581632 | tf_op jit(solution)/shard_map/slice | solution.py:38
  83.9 13.9 %collective-permute-start = (f32[72,8,1]{2,1,0:T(8,128)S(1)}, f32[72,8,1]{2,1,0:T(8,128)S(1)}, u32[]{:S(2)}, u32[]{:S(2)}) collective-permute-start(f32[72,8,1]{2,1,0:T(8,128)S(1)} %get-tuple-element.486), channel_id=1, source_target_pairs={{0,4},{4,8},{8,12},{12,16},{16,20},{20,24},{24,28},{28,0},{1,5},{5... | collective-permute-start | bytes 6920 | tf_op jit(solution)/shard_map/ppermute | solution.py:16
  84.7 15.3 %collective-permute-start.1 = (f32[72,8,1]{2,1,0:T(8,128)S(1)}, f32[72,8,1]{2,1,0:T(8,128)S(1)}, u32[]{:S(2)}, u32[]{:S(2)}) collective-permute-start(f32[72,8,1]{2,1,0:T(8,128)S(1)} %get-tuple-element.487), channel_id=1, source_target_pairs={{4,0},{8,4},{12,8},{16,12},{20,16},{24,20},{28,24},{0,28},{5,1},{9... | collective-permute-start | bytes 6920 | tf_op jit(solution)/shard_map/ppermute | solution.py:17
  100.5 4.5 %copy-start.2 = (f32[72,8,128]{2,1,0:T(8,128)S(1)}, f32[72,8,128]{2,1,0:T(8,128)}, u32[]{:S(2)}) copy-start(f32[72,8,128]{2,1,0:T(8,128)} %param.26) | copy-start | bytes 884740
  100.5 4.5 %copy-start.3 = (f32[72,8,128]{2,1,0:T(8,128)S(1)}, f32[72,8,128]{2,1,0:T(8,128)}, u32[]{:S(2)}) copy-start(f32[72,8,128]{2,1,0:T(8,128)} %param.25) | copy-start | bytes 884740
  100.6 3.8 %collective-permute-start.2 = (f32[72,1,130]{2,1,0:T(1,128)S(1)}, f32[72,1,130]{2,1,0:T(1,128)S(1)}, u32[]{:S(2)}, u32[]{:S(2)}) collective-permute-start(f32[72,1,130]{2,1,0:T(1,128)S(1)} %get-tuple-element.480), channel_id=1, source_target_pairs={{0,1},{1,2},{2,3},{3,0},{4,5},{5,6},{6,7},{7,4},{8,9},{9,10},{10,1... | collective-permute-start | bytes 112328 | tf_op jit(solution)/shard_map/ppermute | solution.py:16
  100.6 3.8 %collective-permute-start.3 = (f32[72,1,130]{2,1,0:T(1,128)S(1)}, f32[72,1,130]{2,1,0:T(1,128)S(1)}, u32[]{:S(2)}, u32[]{:S(2)}) collective-permute-start(f32[72,1,130]{2,1,0:T(1,128)S(1)} %get-tuple-element.481), channel_id=1, source_target_pairs={{1,0},{2,1},{3,2},{0,3},{5,4},{6,5},{7,6},{4,7},{9,8},{10,9},{11,1... | collective-permute-start | bytes 112328 | tf_op jit(solution)/shard_map/ppermute | solution.py:17
  108.3 7.5 %copy-start.5 = (s32[8,128]{1,0:T(8,128)S(1)}, s32[8,128]{1,0:T(8,128)}, u32[]{:S(2)}) copy-start(s32[8,128]{1,0:T(8,128)} %param.28) | copy-start | bytes 12292
  111.1 13.9 %collective-permute-start.4 = (f32[72,8,1]{2,1,0:T(8,128)S(1)}, f32[72,8,1]{2,1,0:T(8,128)S(1)}, u32[]{:S(2)}, u32[]{:S(2)}) collective-permute-start(f32[72,8,1]{2,1,0:T(8,128)S(1)} %get-tuple-element.484), channel_id=1, source_target_pairs={{0,4},{4,8},{8,12},{12,16},{16,20},{20,24},{24,28},{28,0},{1,5},{5... | collective-permute-start | bytes 6920 | tf_op jit(solution)/shard_map/ppermute | solution.py:16
  111.4 16.0 %collective-permute-start.5 = (f32[72,8,1]{2,1,0:T(8,128)S(1)}, f32[72,8,1]{2,1,0:T(8,128)S(1)}, u32[]{:S(2)}, u32[]{:S(2)}) collective-permute-start(f32[72,8,1]{2,1,0:T(8,128)S(1)} %get-tuple-element.485), channel_id=1, source_target_pairs={{4,0},{8,4},{12,8},{16,12},{20,16},{24,20},{28,24},{0,28},{5,1},{9... | collective-permute-start | bytes 6920 | tf_op jit(solution)/shard_map/ppermute | solution.py:17
  122.0 14.2 %copy-start.6 = (s32[1024]{0:T(1024)}, s32[1024]{0:T(1024)S(1)}, u32[]{:S(2)}) copy-start(s32[1024]{0:T(1024)S(1)} %gather_fusion) | copy-start | bytes 12292
  127.9 7.7 %collective-permute-start.6 = (f32[72,1,130]{2,1,0:T(1,128)S(1)}, f32[72,1,130]{2,1,0:T(1,128)S(1)}, u32[]{:S(2)}, u32[]{:S(2)}) collective-permute-start(f32[72,1,130]{2,1,0:T(1,128)S(1)} %get-tuple-element.478), channel_id=1, source_target_pairs={{0,1},{1,2},{2,3},{3,0},{4,5},{5,6},{6,7},{7,4},{8,9},{9,10},{10,1... | collective-permute-start | bytes 112328 | tf_op jit(solution)/shard_map/ppermute | solution.py:16
  127.9 7.7 %collective-permute-start.7 = (f32[72,1,130]{2,1,0:T(1,128)S(1)}, f32[72,1,130]{2,1,0:T(1,128)S(1)}, u32[]{:S(2)}, u32[]{:S(2)}) collective-permute-start(f32[72,1,130]{2,1,0:T(1,128)S(1)} %get-tuple-element.479), channel_id=1, source_target_pairs={{1,0},{2,1},{3,2},{0,3},{5,4},{6,5},{7,6},{4,7},{9,8},{10,9},{11,1... | collective-permute-start | bytes 112328 | tf_op jit(solution)/shard_map/ppermute | solution.py:17
  142.2 8.1 %copy-start.4 = (f32[72,8,128]{2,1,0:T(8,128)}, f32[72,8,128]{2,1,0:T(8,128)S(1)}, u32[]{:S(2)}) copy-start(f32[72,8,128]{2,1,0:T(8,128)S(1)} %get-tuple-element.302) | copy-start | bytes 884740
Sparse Core Ops, SparseCore 0:
  150.5 134.3 reduce-scatter.3
where the time goes:
time: 294 us; the launch traced here: 293 us
  waiting for transfers between devices  174 us (59%)
  other arithmetic  47.2 us (16%)
  starting transfers between devices  33.6 us (11%)
  local copies, waits for them, and re-layouts  16.7 us (6%)
  between operations  15.1 us (5%)
  loops' own time  6.82 us (2%)
    unnamed x2, waiting for transfers between devices  135 us
    ppermute x4, waiting for transfers between devices, with_halo(): before = lax.ppermute(last, axis, up)  13.9 us
    scatter-add x2, other arithmetic, region_partial(): jax.ops.segment_sum(surface.reshape(-1), positions, num_segments=regions)  12 us
    ppermute x4, starting transfers between devices, with_halo(): after = lax.ppermute(leading, axis, down)  11.9 us
    all_to_all x1, waiting for transfers between devices, body(): lax.all_to_all(send_rows, 'lon', split_axis=0, concat_axis=0, tiled=True)  10.7 us
    scatter-add x1, other arithmetic, body(): jax.ops.segment_sum(got_rows, got_code, num_segments=STEPS * cells)  9.79 us
    all_to_all x1, starting transfers between devices, body(): lax.all_to_all(send_code, 'lon', split_axis=0, concat_axis=0, tiled=True)  7.45 us
    all_to_all x1, waiting for transfers between devices, body(): lax.all_to_all(lax.all_to_all(send_rows, 'lon', split_axis=0, concat_axis...  7.03 us
  transfers between devices with their start and end apart: 13, of which 9 were waited for; matrix products, arithmetic and copies ran while one was open for 8% of the time, Pallas kernels for 0%

commit v1 on v0

--- a/solution.py
+++ b/solution.py
@@ -1,6 +1,10 @@
+import functools
+
 import jax
 import jax.numpy as jnp
 from jax import lax
+from jax.experimental import pallas as pl
+from jax.experimental.pallas import tpu as pltpu
 from jax.sharding import PartitionSpec as P
 
 STEPS = 2
@@ -65,7 +69,7 @@
     return ((inside >= 0) & (inside < limit)).astype(jnp.float32)[:, None]
 
 
-def body(
+def general_body(
     sounding_kernel,
     sounding_misfit,
     sounding_owner,
@@ -143,6 +147,482 @@
     return (field, totals)
 
 
+MESH = pl.DeviceIdType.MESH
+F32 = jnp.float32
+BF16 = jnp.bfloat16
+I32 = jnp.int32
+
+
+def iota(shape, dim):
+    return lax.broadcasted_iota(I32, shape, dim)
+
+
+def one_hot(test, dtype=BF16):
+    return jnp.where(test, 1.0, 0.0).astype(dtype)
+
+
+def split(x):
+    high = x.astype(BF16)
+    return high, (x - high.astype(F32)).astype(BF16)
+
+
+def dot_nt(a, b):
+    return lax.dot_general(a, b, (((1,), (1,)), ((), ())), preferred_element_type=F32)
+
+
+def kernel(
+    lat_count,
+    devices,
+    sk_ref,
+    misfit_ref,
+    owner_ref,
+    cell_ref,
+    step_ref,
+    count_ref,
+    cx_ref,
+    cy_ref,
+    dif_ref,
+    map_ref,
+    table_ref,
+    out_ref,
+    reg_ref,
+    target,
+    weights,
+    send,
+    got,
+    dep0,
+    dep1,
+    base,
+    inv,
+    low,
+    up,
+    lon_out,
+    lon_in,
+    lat_out,
+    lat_in,
+    own_hot,
+    loc_hot,
+    part,
+    part_in,
+    a2a_send,
+    a2a_recv,
+    halo_send,
+    halo_recv,
+    reg_send,
+    reg_recv,
+):
+    levels = cx_ref.shape[0]
+    blocks = levels // 8
+    planes = devices // 8
+    half = devices * 16
+    lon = lax.axis_index("lon")
+    lat = lax.axis_index("lat")
+    lon_count = devices // lat_count
+    me = lon * lat_count + lat
+    plane = me // 8
+    inner = me % 8
+
+    def place(peer):
+        return (peer // lat_count, peer % lat_count)
+
+    def flip(value, mask, bits):
+        total = 0
+        for bit in range(bits):
+            v = (value // (1 << bit)) % 2
+            m = (mask // (1 << bit)) % 2
+            total = total + (v + m - 2 * v * m) * (1 << bit)
+        return total
+
+    bits = devices.bit_length() - 1
+    barrier = pltpu.get_barrier_semaphore()
+
+    def greet(d, carry):
+        peer = lax.rem(me + d, devices)
+        pl.semaphore_signal(barrier, inc=1, device_id=place(peer), device_id_type=MESH)
+        return carry
+
+    lax.fori_loop(1, devices, greet, 0)
+
+    lane1 = iota((1, 128), 1)
+    owner_iota = iota((devices, 128), 0)
+    hots, valids, owners = [], [], []
+    count = count_ref[0]
+    for c in range(8):
+        valid = (lane1 + c * 128) < count
+        row = owner_ref[c : c + 1, :]
+        hots.append(one_hot(jnp.where(valid, row, -1) == owner_iota, F32))
+        valids.append(valid)
+        owners.append(row)
+    earlier = one_hot((iota((128, 256), 0) < iota((128, 256), 1)))
+    ranks = jnp.dot(
+        jnp.concatenate(hots, axis=0).astype(BF16), earlier, preferred_element_type=F32
+    )
+    carry = jnp.zeros((devices, 128), F32)
+    for c in range(8):
+        part_c = ranks[c * devices : (c + 1) * devices]
+        rank = jnp.sum(hots[c] * (part_c[:, :128] + carry), axis=0, keepdims=True).astype(I32)
+        carry = carry + part_c[:, 128:]
+        spot = (rank // 16) * half + owners[c] * 16 + rank % 16
+        target[c : c + 1, :] = jnp.where(valids[c], spot, -1)
+
+    for c in range(8):
+        at = slice(c * 128, (c + 1) * 128)
+        forcing = sk_ref[:, at] * misfit_ref[c : c + 1, :]
+        code = (step_ref[c : c + 1, :] * 1024 + cell_ref[c : c + 1, :]).astype(F32)
+        code = jnp.broadcast_to(code, (8, 128))
+        for h in range(2):
+            if h == 0:
+                rest = forcing[:40]
+            else:
+                rest = jnp.concatenate([forcing[40:], jnp.zeros((8, 128), F32)], axis=0)
+            high, small = split(jnp.concatenate([forcing, code, rest, code], axis=0))
+            weights[h, 0:128, at] = high
+            weights[h, 128:256, at] = small
+
+    pl.semaphore_wait(barrier, devices - 1)
+
+    sub128 = iota((128, 128), 0)
+    lane128 = iota((128, 128), 1)
+    order = [2, 3, 1, 0]
+
+    def select_rows(first):
+        return jnp.concatenate(
+            [one_hot(target[c : c + 1, :] - first == sub128) for c in range(8)], axis=1
+        )
+
+    for x in order:
+        there = flip(plane, x, bits - 3)
+        rows = pl.ds(pl.multiple_of(there * 128, 128), 128)
+        late = select_rows(2 * half + there * 128)
+        for h in range(2):
+            picks = jnp.concatenate([select_rows(h * half + there * 128), late], axis=0)
+            both = dot_nt(picks, weights[h])
+            both = both[:, :128] + both[:, 128:]
+            send[h, rows, :] = jnp.where(lane128 < 80, both[:128], both[128:])
+
+        def ship(e, carry, x=x):
+            peer = flip(plane, x, bits - 3) * 8 + flip(inner, e, 3)
+            pltpu.make_async_remote_copy(
+                src_ref=send.at[:, pl.ds(pl.multiple_of(peer * 16, 16), 16), :],
+                dst_ref=got.at[:, pl.ds(pl.multiple_of(me * 16, 16), 16), :],
+                send_sem=a2a_send.at[x],
+                recv_sem=a2a_recv.at[x],
+                device_id=place(peer),
+                device_id_type=MESH,
+            ).start()
+            return carry
+
+        lax.fori_loop(1 if x == 0 else 0, 8, ship, 0)
+    mine = pl.ds(pl.multiple_of(me * 16, 16), 16)
+    got[:, mine, :] = send[:, mine, :]
+
+    def factor(b, carry):
+        k_prev, up_prev = carry
+        for i in range(8):
+            row = pl.ds(pl.multiple_of(b * 64 + i * 8, 8), 8)
+            k_now = dif_ref[b * 8 + i]
+            r = 1.0 / ((1.0 + k_prev + k_now) - k_prev * up_prev)
+            inv[row, :] = r
+            low[row, :] = k_prev * r
+            up_prev = k_now * r
+            up[row, :] = up_prev
+            k_prev = k_now
+        return (k_prev, up_prev)
+
+    zero = jnp.zeros((8, 128), F32)
+    lax.fori_loop(0, blocks, factor, (zero, zero))
+
+    table = table_ref[...]
+    table = jnp.concatenate([table // 128, table % 128], axis=0).astype(F32).astype(BF16)
+    for a in range(8):
+        at = slice(a * 128, (a + 1) * 128)
+        region = map_ref[a : a + 1, :]
+        found = jnp.dot(table, one_hot(region % 128 == sub128), preferred_element_type=F32)
+        pick = one_hot(region // 128 == owner_iota, F32)
+        own = jnp.sum(found[:devices] * pick, axis=0, keepdims=True).astype(I32)
+        loc = jnp.sum(found[devices:] * pick, axis=0, keepdims=True).astype(I32)
+        own_hot[:, at] = one_hot(own == owner_iota, F32)
+        loc_hot[:, at] = one_hot(loc == sub128)
+
+    sub8 = iota((8, 128), 0)
+    lane256 = iota((128, 256), 1)
+
+    def spread(rows, code):
+        mask = one_hot((code // 128) % 8 == sub8, F32)
+        y = (rows[:, None, :] * mask[None]).reshape(levels * 8, 128)
+        return split(y)
+
+    def column(code):
+        return one_hot(code % 128 + (code // 1024) * 128 == lane256)
+
+    for n, x in enumerate(order):
+        there = flip(plane, x, bits - 3)
+        if x == 0:
+            seen = got.at[:, pl.ds(0, 112), :]
+        else:
+            seen = got.at[:, pl.ds(0, 128), :]
+        pltpu.make_async_copy(seen, seen, a2a_recv.at[x]).wait()
+        rows = pl.ds(pl.multiple_of(there * 128, 128), 128)
+        first = got[0, rows, :]
+        second = got[1, rows, :]
+        first_t = first.T
+        second_t = second.T
+        late_t = jnp.concatenate([first_t[80:120], second_t[80:112]], axis=0)
+        left, right = [], []
+        for values, code_row, code_col in (
+            (first_t[:72], first_t[72:73], first[:, 72:73]),
+            (second_t[:72], second_t[72:73], second[:, 72:73]),
+            (late_t, first_t[120:121], first[:, 120:121]),
+        ):
+            left.extend(spread(values, code_row.astype(I32)))
+            right.extend([column(code_col.astype(I32))] * 2)
+        total = jnp.dot(
+            jnp.concatenate(left, axis=1),
+            jnp.concatenate(right, axis=0),
+            preferred_element_type=F32,
+        )
+        if n == 0:
+            dep0[...] = total[:, :128]
+            dep1[...] = total[:, 128:]
+        else:
+            dep0[...] += total[:, :128]
+            dep1[...] += total[:, 128:]
+
+    lane8 = iota((8, 128), 1)
+    east = (lax.rem(lon + 1, lon_count), lat)
+    west = (lax.rem(lon + lon_count - 1, lon_count), lat)
+    north = (lon, lax.rem(lat + 1, lat_count))
+    south = (lon, lax.rem(lat + lat_count - 1, lat_count))
+    has_south = (lat > 0).astype(F32)
+    has_north = (lat < lat_count - 1).astype(F32)
+
+    def region_part(surface, step):
+        spread_rows = jnp.concatenate(
+            [own_hot[:, a * 128 : (a + 1) * 128] * surface[a : a + 1] for a in range(8)], axis=1
+        )
+        both = dot_nt(jnp.concatenate(split(spread_rows), axis=0), loc_hot[...])
+        total = both[:devices] + both[devices:]
+        for o in range(devices):
+            part[o, step : step + 1, :] = total[o : o + 1]
+
+    surface = None
+    for step in range(STEPS):
+        def gather(n, carry):
+            first, last = carry
+            b = blocks - 1 - n
+            first = pltpu.roll(first, 8, 1)
+            last = pltpu.roll(last, 8, 1)
+            for i in range(8):
+                x = dep0[pl.ds(pl.multiple_of(b * 64 + i * 8, 8), 8), :]
+                first = jnp.where(lane8 == i, pltpu.roll(x, i, 1) if i else x, first)
+                last = jnp.where(lane8 == i, pltpu.roll(x, i + 1, 1), last)
+            return (first, last)
+
+        first, last = lax.fori_loop(0, blocks, gather, (zero, zero))
+        lon_out[step, 0] = first
+        lon_out[step, 1] = last
+        lat_out[step, 0] = dep0[pl.ds(0, levels, stride=8), :]
+        lat_out[step, 1] = dep0[pl.ds(7, levels, stride=8), :]
+        copies = []
+        for n, (src, dst, to) in enumerate(
+            (
+                (lat_out.at[step, 0], lat_in.at[step, 1], south),
+                (lat_out.at[step, 1], lat_in.at[step, 0], north),
+                (lon_out.at[step, 0], lon_in.at[step, 1], west),
+                (lon_out.at[step, 1], lon_in.at[step, 0], east),
+            )
+        ):
+            copy = pltpu.make_async_remote_copy(
+                src_ref=src,
+                dst_ref=dst,
+                send_sem=halo_send.at[step, n],
+                recv_sem=halo_recv.at[step, n],
+                device_id=to,
+                device_id_type=MESH,
+            )
+            copy.start()
+            copies.append(copy)
+
+        def inside(b, carry):
+            for i in range(8):
+                row = pl.ds(pl.multiple_of(b * 64 + i * 8, 8), 8)
+                x = dep0[row, :]
+                cx = cx_ref[b * 8 + i]
+                cy = cy_ref[b * 8 + i]
+                to_west = jnp.where(lane8 == 0, 0.0, pltpu.roll(x, 1, 1))
+                to_east = jnp.where(lane8 == 127, 0.0, pltpu.roll(x, 127, 1))
+                to_south = jnp.where(sub8 == 0, 0.0, pltpu.roll(x, 1, 0))
+                to_north = jnp.where(sub8 == 7, 0.0, pltpu.roll(x, 7, 0))
+                base[row, :] = (
+                    x
+                    - jnp.maximum(cx, 0.0) * (x - to_west)
+                    - jnp.maximum(-cx, 0.0) * (x - to_east)
+                    - jnp.maximum(cy, 0.0) * (x - to_south)
+                    - jnp.maximum(-cy, 0.0) * (x - to_north)
+                )
+            return carry
+
+        lax.fori_loop(0, blocks, inside, 0)
+        if step > 0:
+            region_part(surface, step - 1)
+        for copy in copies:
+            copy.wait()
+
+        def forward(b, carry):
+            g, from_west, from_east = carry
+            eight = pl.ds(pl.multiple_of(b * 8, 8), 8)
+            from_south = lat_in[step, 0, eight, :] * has_south
+            from_north = lat_in[step, 1, eight, :] * has_north
+            for i in range(8):
+                row = pl.ds(pl.multiple_of(b * 64 + i * 8, 8), 8)
+                cx = cx_ref[b * 8 + i]
+                cy = cy_ref[b * 8 + i]
+                w = pltpu.roll(from_west, 128 - i, 1) if i else from_west
+                e = pltpu.roll(from_east, 127 - i, 1)
+                x_edge = jnp.where(
+                    lane8 == 0,
+                    jnp.maximum(cx, 0.0) * w,
+                    jnp.where(lane8 == 127, jnp.maximum(-cx, 0.0) * e, 0.0),
+                )
+                y_edge = jnp.where(
+                    sub8 == 0,
+                    jnp.maximum(cy, 0.0) * from_south[i : i + 1],
+                    jnp.where(sub8 == 7, jnp.maximum(-cy, 0.0) * from_north[i : i + 1], 0.0),
+                )
+                rhs = base[row, :] + x_edge + y_edge
+                g = rhs * inv[row, :] + low[row, :] * g
+                base[row, :] = g
+            return (g, pltpu.roll(from_west, 120, 1), pltpu.roll(from_east, 120, 1))
+
+        lax.fori_loop(0, blocks, forward, (zero, lon_in[step, 0], lon_in[step, 1]))
+
+        def backward(n, x):
+            b = blocks - 1 - n
+            for i in reversed(range(8)):
+                row = pl.ds(pl.multiple_of(b * 64 + i * 8, 8), 8)
+                x = base[row, :] + up[row, :] * x
+                if step < STEPS - 1:
+                    dep0[row, :] = x + dep1[row, :]
+                else:
+                    out_ref[b * 8 + i] = x
+            return x
+
+        surface = lax.fori_loop(0, blocks, backward, zero)
+
+    region_part(surface, STEPS - 1)
+
+    def hand_out(d, carry):
+        peer = lax.rem(me + d, devices)
+        pltpu.make_async_remote_copy(
+            src_ref=part.at[peer],
+            dst_ref=part_in.at[me],
+            send_sem=reg_send,
+            recv_sem=reg_recv,
+            device_id=place(peer),
+            device_id_type=MESH,
+        ).start()
+        return carry
+
+    lax.fori_loop(1, devices, hand_out, 0)
+    part_in[me] = part[me]
+    others = part_in.at[pl.ds(0, devices - 1)]
+    pltpu.make_async_copy(others, others, reg_recv).wait()
+    reg_ref[...] = jnp.sum(part_in[...], axis=0)
+
+    others = part.at[pl.ds(0, devices - 1)]
+    pltpu.make_async_copy(others, others, reg_send).wait()
+    for x in order:
+        seen = send.at[:, pl.ds(0, 112 if x == 0 else 128), :]
+        pltpu.make_async_copy(seen, seen, a2a_send.at[x]).wait()
+
+
+def body(
+    sounding_kernel,
+    sounding_misfit,
+    sounding_owner,
+    sounding_cell,
+    sounding_step,
+    sounding_count,
+    courant_x,
+    courant_y,
+    diffusivity,
+    region_map,
+    region_owner,
+):
+    levels, rows_lat, rows_lon = courant_x.shape
+    lat_count = lax.axis_size("lat")
+    devices = lat_count * lax.axis_size("lon")
+    per_device = sounding_misfit.shape[0]
+    capacity = max(2, 3 * per_device // (2 * devices))
+    if (capacity, devices, levels, rows_lat, rows_lon, per_device) != (48, 32, 72, 8, 128, 1024):
+        return general_body(
+            sounding_kernel,
+            sounding_misfit,
+            sounding_owner,
+            sounding_cell,
+            sounding_step,
+            sounding_count,
+            courant_x,
+            courant_y,
+            diffusivity,
+            region_map,
+            region_owner,
+        )
+    vmem = pl.BlockSpec(memory_space=pltpu.VMEM)
+    smem = pl.BlockSpec(memory_space=pltpu.SMEM)
+    cells = (levels * rows_lat, rows_lon)
+    return pl.pallas_call(
+        functools.partial(kernel, lat_count, devices),
+        out_shape=(
+            jax.ShapeDtypeStruct(courant_x.shape, F32),
+            jax.ShapeDtypeStruct((STEPS, 128), F32),
+        ),
+        in_specs=[vmem] * 5 + [smem] + [vmem] * 5,
+        out_specs=(vmem, vmem),
+        scratch_shapes=[
+            pltpu.VMEM((8, 128), I32),
+            pltpu.VMEM((2, 256, per_device), BF16),
+            pltpu.VMEM((2, devices * 16, 128), F32),
+            pltpu.VMEM((2, devices * 16, 128), F32),
+            pltpu.VMEM(cells, F32),
+            pltpu.VMEM(cells, F32),
+            pltpu.VMEM(cells, F32),
+            pltpu.VMEM(cells, F32),
+            pltpu.VMEM(cells, F32),
+            pltpu.VMEM(cells, F32),
+            pltpu.VMEM((STEPS, 2, 8, 128), F32),
+            pltpu.VMEM((STEPS, 2, 8, 128), F32),
+            pltpu.VMEM((STEPS, 2, levels, 128), F32),
+            pltpu.VMEM((STEPS, 2, levels, 128), F32),
+            pltpu.VMEM((devices, 1024), F32),
+            pltpu.VMEM((128, 1024), BF16),
+            pltpu.VMEM((devices, STEPS, 128), F32),
+            pltpu.VMEM((devices, STEPS, 128), F32),
+            pltpu.SemaphoreType.DMA((4,)),
+            pltpu.SemaphoreType.DMA((4,)),
+            pltpu.SemaphoreType.DMA((STEPS, 4)),
+            pltpu.SemaphoreType.DMA((STEPS, 4)),
+            pltpu.SemaphoreType.DMA,
+            pltpu.SemaphoreType.DMA,
+        ],
+        compiler_params=pltpu.CompilerParams(
+            collective_id=0, has_side_effects=True, vmem_limit_bytes=40 * 1024 * 1024
+        ),
+    )(
+        sounding_kernel,
+        sounding_misfit.reshape(8, 128),
+        sounding_owner.reshape(8, 128),
+        sounding_cell.reshape(8, 128),
+        sounding_step.reshape(8, 128),
+        sounding_count,
+        courant_x,
+        courant_y,
+        diffusivity,
+        region_map,
+        region_owner.reshape(-1, 128),
+    )
+
+
 def solution(mesh):
     placed = (
         P(None, ("lon", "lat")),

time: 294 us -> 48.3 us (0.16)
  waiting for transfers between devices: 174 us -> 0 us
  other arithmetic: 47.2 us -> 0 us
  Pallas kernels: 0 us -> 38 us
  starting transfers between devices: 33.6 us -> 0 us
  between operations: 15.1 us -> 1.31 us
  local copies, waits for them, and re-layouts: 16.7 us -> 8.59 us
  loops' own time: 6.82 us -> 0 us
    unnamed x2 -> x0, waiting for transfers between devices: 135 us -> none
    pallas_call x0 -> x1, Pallas kernels: none -> 38 us  [body(): pl.pallas_call(functools.partial(kernel, lat_count, devices), out_shape=(...]
    scatter-add x5 -> x0, other arithmetic: 34.2 us -> none  [the longest x2 12 us: region_partial(): jax.ops.segment_sum(surface.reshape(-1), positions, num_segments=regions)]
    all_to_all x4 -> x0, waiting for transfers between devices: 20.7 us -> none  [the longest x1 10.7 us: body(): lax.all_to_all(send_rows, 'lon', split_axis=0, concat_axis=0, tiled=True)]
    all_to_all x4 -> x0, starting transfers between devices: 20.4 us -> none  [the longest x1 7.45 us: body(): lax.all_to_all(send_code, 'lon', split_axis=0, concat_axis=0, tiled=True)]
    ppermute x8 -> x0, waiting for transfers between devices: 18.5 us -> none  [the longest x4 13.9 us: with_halo(): before = lax.ppermute(last, axis, up)]
    ppermute x8 -> x0, starting transfers between devices: 13.1 us -> none  [the longest x4 11.9 us: with_halo(): after = lax.ppermute(leading, axis, down)]
    another operation x4 -> x0, loops' own time: 6.82 us -> none  [the longest x2 3.41 us: diffuse(): _, solved = lax.scan(backward, zero, (w_all, g_all), reverse=True)]
  transfers between devices with their start and end apart: 13 -> 0, of which waited for: 9 -> 0; matrix products, arithmetic and copies ran while one was open for 8% -> 0% of each run, Pallas kernels for 0% -> 0%
where the time goes in v1:
time: 48.3 us; the launch traced here: 47.9 us
  Pallas kernels  38 us (79%)
  local copies, waits for them, and re-layouts  8.59 us (18%)
  between operations  1.31 us (3%)
    pallas_call x1, Pallas kernels, body(): pl.pallas_call(functools.partial(kernel, lat_count, devices), out_shape=(...  38 us
    unnamed x22, local copies, waits for them, and re-layouts  8.59 us

profile of v1, /device:TPU:0, one launch (start us, length us, event | category | flops | bytes accessed | tf_op | source)
XLA Modules:
  0.0 47.9 jit_solution(13342260437528954973)
XLA Ops:
  1.3 0.0 copy-start.6
  1.3 0.0 copy-start.5
  1.3 0.7 %copy-done.6 = s32[1024,1]{0,1:T(1,128)S(1)} copy-done((s32[1024,1]{0,1:T(1,128)S(1)}, s32[1024,1]{0,1:T(1,128)}, u32[]{:S(2)}) %copy-start.6) | copy-done | bytes 4120
  2.0 0.0 copy-done.5
  2.0 0.0 copy-start
  2.0 1.0 %copy-done = f32[72,1024]{1,0:T(8,128)S(1)} copy-done((f32[72,1024]{1,0:T(8,128)S(1)}, f32[72,1024]{1,0:T(8,128)}, u32[]{:S(2)}) %copy-start) | copy-done | bytes 294936
  2.9 0.0 copy-start.1
  2.9 1.0 %copy-done.1 = f32[72,8,128]{2,1,0:T(8,128)S(1)} copy-done((f32[72,8,128]{2,1,0:T(8,128)S(1)}, f32[72,8,128]{2,1,0:T(8,128)}, u32[]{:S(2)}) %copy-start.1) | copy-done | bytes 294936
  3.9 0.0 copy-start.2
  3.9 1.0 %copy-done.2 = f32[72,8,128]{2,1,0:T(8,128)S(1)} copy-done((f32[72,8,128]{2,1,0:T(8,128)S(1)}, f32[72,8,128]{2,1,0:T(8,128)}, u32[]{:S(2)}) %copy-start.2) | copy-done | bytes 294936
  4.9 0.0 copy-start.3
  4.9 1.0 %copy-done.3 = f32[72,8,128]{2,1,0:T(8,128)S(1)} copy-done((f32[72,8,128]{2,1,0:T(8,128)S(1)}, f32[72,8,128]{2,1,0:T(8,128)}, u32[]{:S(2)}) %copy-start.3) | copy-done | bytes 294936
  5.8 0.0 copy-start.4
  5.8 0.7 %copy-done.4 = s32[4096]{0:T(1024)S(1)} copy-done((s32[4096]{0:T(1024)S(1)}, s32[4096]{0:T(1024)}, u32[]{:S(2)}) %copy-start.4) | copy-done | bytes 16408
  6.5 0.0 copy-start.7
  6.6 0.7 %copy-done.7 = s32[1024]{0:T(1024)S(1)} copy-done((s32[1024]{0:T(1024)S(1)}, s32[1024]{0:T(1024)}, u32[]{:S(2)}) %copy-start.7) | copy-done | bytes 4120
  7.2 0.0 copy-start.8
  7.2 0.7 %copy-done.8 = s32[1024]{0:T(1024)S(1)} copy-done((s32[1024]{0:T(1024)S(1)}, s32[1024]{0:T(1024)}, u32[]{:S(2)}) %copy-start.8) | copy-done | bytes 4120
  7.9 0.0 copy-start.9
  7.9 0.7 %copy-done.9 = s32[8,128]{1,0:T(8,128)S(1)} copy-done((s32[8,128]{1,0:T(8,128)S(1)}, s32[8,128]{1,0:T(8,128)}, u32[]{:S(2)}) %copy-start.9) | copy-done | bytes 4120
  8.6 38.0 %shard_map.122 = (f32[72,8,128]{2,1,0:T(8,128)S(1)}, f32[2,128]{1,0:T(2,128)S(1)}) custom-call(f32[72,1024]{1,0:T(8,128)S(1)} %copy-done, f32[8,128]{1,0:T(8,128)S(1)} %bitcast.6, s32[8,128]{1,0:T(8,128)S(1)} %bitcast.7, s32[8,128]{1,0:T(8,128)S(1)} %bitcast.8, s32[8,128]{1,0:T(8,128)S(1)} %bitcast.9, s32[1]{0:T(128)S(6)} %copy.15.count_ref, ...), custom_call_target="tpu_custom_call" | custom-call | tf_op jit(solution)/shard_map/pallas_call | solution.py:574
  46.6 0.7 %copy.16 = f32[72,8,128]{2,1,0:T(8,128)} copy(f32[72,8,128]{2,1,0:T(8,128)S(1)} %get-tuple-element.4) | data formatting | bytes 589824
  47.3 0.6 %copy.17 = f32[2,128]{1,0:T(2,128)} copy(f32[2,128]{1,0:T(2,128)S(1)} %get-tuple-element.5) | data formatting | bytes 2048
Async XLA Ops:
  1.3 0.7 %copy-start.6 = (s32[1024,1]{0,1:T(1,128)S(1)}, s32[1024,1]{0,1:T(1,128)}, u32[]{:S(2)}) copy-start(s32[1024,1]{0,1:T(1,128)} %param.13) | copy-start | bytes 12292
  1.3 0.7 %copy-start.5 = (f32[1024]{0:T(1024)S(1)}, f32[1024]{0:T(1024)}, u32[]{:S(2)}) copy-start(f32[1024]{0:T(1024)} %param.12) | copy-start | bytes 12292
  2.0 1.0 %copy-start = (f32[72,1024]{1,0:T(8,128)S(1)}, f32[72,1024]{1,0:T(8,128)}, u32[]{:S(2)}) copy-start(f32[72,1024]{1,0:T(8,128)} %sk_ref.1) | copy-start | bytes 884740
  2.9 1.0 %copy-start.1 = (f32[72,8,128]{2,1,0:T(8,128)S(1)}, f32[72,8,128]{2,1,0:T(8,128)}, u32[]{:S(2)}) copy-start(f32[72,8,128]{2,1,0:T(8,128)} %cx_ref.1) | copy-start | bytes 884740
  3.9 1.0 %copy-start.2 = (f32[72,8,128]{2,1,0:T(8,128)S(1)}, f32[72,8,128]{2,1,0:T(8,128)}, u32[]{:S(2)}) copy-start(f32[72,8,128]{2,1,0:T(8,128)} %cy_ref.1) | copy-start | bytes 884740
  4.9 1.0 %copy-start.3 = (f32[72,8,128]{2,1,0:T(8,128)S(1)}, f32[72,8,128]{2,1,0:T(8,128)}, u32[]{:S(2)}) copy-start(f32[72,8,128]{2,1,0:T(8,128)} %dif_ref.1) | copy-start | bytes 884740
  5.8 0.7 %copy-start.4 = (s32[4096]{0:T(1024)S(1)}, s32[4096]{0:T(1024)}, u32[]{:S(2)}) copy-start(s32[4096]{0:T(1024)} %param.21) | copy-start | bytes 49156
  6.5 0.7 %copy-start.7 = (s32[1024]{0:T(1024)S(1)}, s32[1024]{0:T(1024)}, u32[]{:S(2)}) copy-start(s32[1024]{0:T(1024)} %param.14) | copy-start | bytes 12292
  7.2 0.7 %copy-start.8 = (s32[1024]{0:T(1024)S(1)}, s32[1024]{0:T(1024)}, u32[]{:S(2)}) copy-start(s32[1024]{0:T(1024)} %param.15) | copy-start | bytes 12292
  7.9 0.7 %copy-start.9 = (s32[8,128]{1,0:T(8,128)S(1)}, s32[8,128]{1,0:T(8,128)}, u32[]{:S(2)}) copy-start(s32[8,128]{1,0:T(8,128)} %map_ref.1) | copy-start | bytes 12292

commit v2 on v1

--- a/solution.py
+++ b/solution.py
@@ -173,19 +173,30 @@
 def kernel(
     lat_count,
     devices,
+    sk_hbm,
+    misfit_hbm,
+    owner_hbm,
+    cell_hbm,
+    step_hbm,
+    count_ref,
+    cx_hbm,
+    cy_hbm,
+    dif_hbm,
+    map_hbm,
+    table_hbm,
+    out_ref,
+    reg_ref,
     sk_ref,
     misfit_ref,
     owner_ref,
     cell_ref,
     step_ref,
-    count_ref,
     cx_ref,
     cy_ref,
     dif_ref,
     map_ref,
     table_ref,
-    out_ref,
-    reg_ref,
+    load_sem,
     target,
     weights,
     send,
@@ -219,30 +230,46 @@
     lat = lax.axis_index("lat")
     lon_count = devices // lat_count
     me = lon * lat_count + lat
-    plane = me // 8
-    inner = me % 8
-
-    def place(peer):
-        return (peer // lat_count, peer % lat_count)
-
-    def flip(value, mask, bits):
-        total = 0
-        for bit in range(bits):
-            v = (value // (1 << bit)) % 2
-            m = (mask // (1 << bit)) % 2
-            total = total + (v + m - 2 * v * m) * (1 << bit)
-        return total
-
-    bits = devices.bit_length() - 1
+
+    def flips(value, size):
+        digits = [(value // (1 << k)) % 2 for k in range(size.bit_length() - 1)]
+        return [
+            sum((1 - d if mask >> k & 1 else d) * (1 << k) for k, d in enumerate(digits))
+            for mask in range(size)
+        ]
+
+    lons = flips(lon, lon_count)
+    lats = flips(lat, lat_count)
+
+    def place(mask):
+        return (lons[mask // lat_count], lats[mask % lat_count])
+
+    def number(mask):
+        return lons[mask // lat_count] * lat_count + lats[mask % lat_count]
+
+    loads = {}
+    for n, (name, src, dst) in enumerate(
+        (
+            ("owner", owner_hbm, owner_ref),
+            ("misfit", misfit_hbm, misfit_ref),
+            ("cell", cell_hbm, cell_ref),
+            ("step", step_hbm, step_ref),
+            ("sk", sk_hbm, sk_ref),
+            ("dif", dif_hbm, dif_ref),
+            ("map", map_hbm, map_ref),
+            ("table", table_hbm, table_ref),
+            ("cx", cx_hbm, cx_ref),
+            ("cy", cy_hbm, cy_ref),
+        )
+    ):
+        loads[name] = pltpu.make_async_copy(src, dst, load_sem.at[n])
+        loads[name].start()
     barrier = pltpu.get_barrier_semaphore()
 
-    def greet(d, carry):
-        peer = lax.rem(me + d, devices)
-        pl.semaphore_signal(barrier, inc=1, device_id=place(peer), device_id_type=MESH)
-        return carry
-
-    lax.fori_loop(1, devices, greet, 0)
-
+    for mask in range(1, devices):
+        pl.semaphore_signal(barrier, inc=1, device_id=place(mask), device_id_type=MESH)
+
+    loads["owner"].wait()
     lane1 = iota((1, 128), 1)
     owner_iota = iota((devices, 128), 0)
     hots, valids, owners = [], [], []
@@ -265,6 +292,8 @@
         spot = (rank // 16) * half + owners[c] * 16 + rank % 16
         target[c : c + 1, :] = jnp.where(valids[c], spot, -1)
 
+    for name in ("misfit", "cell", "step", "sk"):
+        loads[name].wait()
     for c in range(8):
         at = slice(c * 128, (c + 1) * 128)
         forcing = sk_ref[:, at] * misfit_ref[c : c + 1, :]
@@ -279,11 +308,10 @@
             weights[h, 0:128, at] = high
             weights[h, 128:256, at] = small
 
-    pl.semaphore_wait(barrier, devices - 1)
-
     sub128 = iota((128, 128), 0)
     lane128 = iota((128, 128), 1)
     order = [2, 3, 1, 0]
+    arrival = [0, 1, 3, 2]
 
     def select_rows(first):
         return jnp.concatenate(
@@ -291,7 +319,7 @@
         )
 
     for x in order:
-        there = flip(plane, x, bits - 3)
+        there = number(x * 8) // 8
         rows = pl.ds(pl.multiple_of(there * 128, 128), 128)
         late = select_rows(2 * half + there * 128)
         for h in range(2):
@@ -300,19 +328,18 @@
             both = both[:, :128] + both[:, 128:]
             send[h, rows, :] = jnp.where(lane128 < 80, both[:128], both[128:])
 
-        def ship(e, carry, x=x):
-            peer = flip(plane, x, bits - 3) * 8 + flip(inner, e, 3)
+        if x == order[0]:
+            pl.semaphore_wait(barrier, devices - 1)
+        for mask in range(max(1, x * 8), x * 8 + 8):
+            peer = number(mask)
             pltpu.make_async_remote_copy(
                 src_ref=send.at[:, pl.ds(pl.multiple_of(peer * 16, 16), 16), :],
                 dst_ref=got.at[:, pl.ds(pl.multiple_of(me * 16, 16), 16), :],
                 send_sem=a2a_send.at[x],
                 recv_sem=a2a_recv.at[x],
-                device_id=place(peer),
+                device_id=place(mask),
                 device_id_type=MESH,
             ).start()
-            return carry
-
-        lax.fori_loop(1 if x == 0 else 0, 8, ship, 0)
     mine = pl.ds(pl.multiple_of(me * 16, 16), 16)
     got[:, mine, :] = send[:, mine, :]
 
@@ -330,8 +357,11 @@
         return (k_prev, up_prev)
 
     zero = jnp.zeros((8, 128), F32)
+    loads["dif"].wait()
     lax.fori_loop(0, blocks, factor, (zero, zero))
 
+    loads["map"].wait()
+    loads["table"].wait()
     table = table_ref[...]
     table = jnp.concatenate([table // 128, table % 128], axis=0).astype(F32).astype(BF16)
     for a in range(8):
@@ -355,8 +385,8 @@
     def column(code):
         return one_hot(code % 128 + (code // 1024) * 128 == lane256)
 
-    for n, x in enumerate(order):
-        there = flip(plane, x, bits - 3)
+    for n, x in enumerate(arrival):
+        there = number(x * 8) // 8
         if x == 0:
             seen = got.at[:, pl.ds(0, 112), :]
         else:
@@ -389,7 +419,7 @@
             dep1[...] += total[:, 128:]
 
     lane8 = iota((8, 128), 1)
-    east = (lax.rem(lon + 1, lon_count), lat)
+    east = ((lon + 1) % lon_count, lat)
     west = (lax.rem(lon + lon_count - 1, lon_count), lat)
     north = (lon, lax.rem(lat + 1, lat_count))
     south = (lon, lax.rem(lat + lat_count - 1, lat_count))
@@ -405,6 +435,8 @@
         for o in range(devices):
             part[o, step : step + 1, :] = total[o : o + 1]
 
+    loads["cx"].wait()
+    loads["cy"].wait()
     surface = None
     for step in range(STEPS):
         def gather(n, carry):
@@ -418,7 +450,7 @@
                 last = jnp.where(lane8 == i, pltpu.roll(x, i + 1, 1), last)
             return (first, last)
 
-        first, last = lax.fori_loop(0, blocks, gather, (zero, zero))
+        first, last = lax.fori_loop(0, blocks, gather, (zero, zero), unroll=True)
         lon_out[step, 0] = first
         lon_out[step, 1] = last
         lat_out[step, 0] = dep0[pl.ds(0, levels, stride=8), :]
@@ -462,7 +494,7 @@
                 )
             return carry
 
-        lax.fori_loop(0, blocks, inside, 0)
+        lax.fori_loop(0, blocks, inside, 0, unroll=True)
         if step > 0:
             region_part(surface, step - 1)
         for copy in copies:
@@ -494,7 +526,8 @@
                 base[row, :] = g
             return (g, pltpu.roll(from_west, 120, 1), pltpu.roll(from_east, 120, 1))
 
-        lax.fori_loop(0, blocks, forward, (zero, lon_in[step, 0], lon_in[step, 1]))
+        edges = (zero, lon_in[step, 0], lon_in[step, 1])
+        lax.fori_loop(0, blocks, forward, edges, unroll=True)
 
         def backward(n, x):
             b = blocks - 1 - n
@@ -507,23 +540,19 @@
                     out_ref[b * 8 + i] = x
             return x
 
-        surface = lax.fori_loop(0, blocks, backward, zero)
+        surface = lax.fori_loop(0, blocks, backward, zero, unroll=True)
 
     region_part(surface, STEPS - 1)
 
-    def hand_out(d, carry):
-        peer = lax.rem(me + d, devices)
+    for mask in reversed(range(1, devices)):
         pltpu.make_async_remote_copy(
-            src_ref=part.at[peer],
+            src_ref=part.at[number(mask)],
             dst_ref=part_in.at[me],
             send_sem=reg_send,
             recv_sem=reg_recv,
-            device_id=place(peer),
+            device_id=place(mask),
             device_id_type=MESH,
         ).start()
-        return carry
-
-    lax.fori_loop(1, devices, hand_out, 0)
     part_in[me] = part[me]
     others = part_in.at[pl.ds(0, devices - 1)]
     pltpu.make_async_copy(others, others, reg_recv).wait()
@@ -569,6 +598,7 @@
             region_owner,
         )
     vmem = pl.BlockSpec(memory_space=pltpu.VMEM)
+    hbm = pl.BlockSpec(memory_space=pltpu.HBM)
     smem = pl.BlockSpec(memory_space=pltpu.SMEM)
     cells = (levels * rows_lat, rows_lon)
     return pl.pallas_call(
@@ -577,9 +607,20 @@
             jax.ShapeDtypeStruct(courant_x.shape, F32),
             jax.ShapeDtypeStruct((STEPS, 128), F32),
         ),
-        in_specs=[vmem] * 5 + [smem] + [vmem] * 5,
+        in_specs=[hbm] * 5 + [smem] + [hbm] * 5,
         out_specs=(vmem, vmem),
         scratch_shapes=[
+            pltpu.VMEM((levels, per_device), F32),
+            pltpu.VMEM((8, 128), F32),
+            pltpu.VMEM((8, 128), I32),
+            pltpu.VMEM((8, 128), I32),
+            pltpu.VMEM((8, 128), I32),
+            pltpu.VMEM(courant_x.shape, F32),
+            pltpu.VMEM(courant_x.shape, F32),
+            pltpu.VMEM(courant_x.shape, F32),
+            pltpu.VMEM((8, 128), I32),
+            pltpu.VMEM((region_owner.shape[0] // 128, 128), I32),
+            pltpu.SemaphoreType.DMA((10,)),
             pltpu.VMEM((8, 128), I32),
             pltpu.VMEM((2, 256, per_device), BF16),
             pltpu.VMEM((2, devices * 16, 128), F32),
@@ -606,7 +647,7 @@
             pltpu.SemaphoreType.DMA,
         ],
         compiler_params=pltpu.CompilerParams(
-            collective_id=0, has_side_effects=True, vmem_limit_bytes=40 * 1024 * 1024
+            collective_id=0, has_side_effects=True, vmem_limit_bytes=56 * 1024 * 1024
         ),
     )(
         sounding_kernel,

time: 48.3 us -> 40.2 us (0.83)
  local copies, waits for them, and re-layouts: 8.59 us -> 2.26 us
  Pallas kernels: 38 us -> 36.4 us
    unnamed x22 -> x4, local copies, waits for them, and re-layouts: 8.59 us -> 2.26 us
    pallas_call x1, Pallas kernels: 38 us -> 36.4 us  [body(): pl.pallas_call(functools.partial(kernel, lat_count, devices), out_shape=(...]
where the time goes in v2:
time: 40.2 us; the launch traced here: 40 us
  Pallas kernels  36.4 us (91%)
  local copies, waits for them, and re-layouts  2.26 us (6%)
  between operations  1.3 us (3%)
    pallas_call x1, Pallas kernels, body(): pl.pallas_call(functools.partial(kernel, lat_count, devices), out_shape=(...  36.4 us
    unnamed x4, local copies, waits for them, and re-layouts  2.26 us

profile of v2, /device:TPU:0, one launch (start us, length us, event | category | flops | bytes accessed | tf_op | source)
XLA Modules:
  0.0 40.0 jit_solution(4992773872278075692)
XLA Ops:
  1.3 36.4 %shard_map.122 = (f32[72,8,128]{2,1,0:T(8,128)}, f32[2,128]{1,0:T(2,128)}) custom-call(f32[72,1024]{1,0:T(8,128)} %sk_hbm.1, f32[8,128]{1,0:T(8,128)} %bitcast.6, s32[8,128]{1,0:T(8,128)} %bitcast.7, s32[8,128]{1,0:T(8,128)} %bitcast.8, s32[8,128]{1,0:T(8,128)} %bitcast.9, s32[1]{0:T(128)S(6)} %copy.15.count_ref, f32[72,8,128]{2,1,0:T(8,128)} %cx_hbm.1, ...), custom_call_target="tpu_custom_call" | custom-call | tf_op jit(solution)/shard_map/pallas_call | solution.py:604
  37.7 0.0 copy-start
  37.7 1.7 %copy.16 = f32[72,8,128]{2,1,0:T(8,128)} copy(f32[72,8,128]{2,1,0:T(8,128)} %get-tuple-element.4) | data formatting | bytes 589824
  39.4 0.0 copy-done
  39.4 0.6 %copy.17 = f32[2,128]{1,0:T(2,128)} copy(f32[2,128]{1,0:T(2,128)S(1)} %copy-done) | data formatting | bytes 2048
Async XLA Ops:
  37.7 1.7 %copy-start = (f32[2,128]{1,0:T(2,128)S(1)}, f32[2,128]{1,0:T(2,128)}, u32[]{:S(2)}) copy-start(f32[2,128]{1,0:T(2,128)} %get-tuple-element.5) | copy-start | bytes 3076

commit v3 on v2

--- a/solution.py
+++ b/solution.py
@@ -184,7 +184,7 @@
     dif_hbm,
     map_hbm,
     table_hbm,
-    out_ref,
+    out_hbm,
     reg_ref,
     sk_ref,
     misfit_ref,
@@ -197,6 +197,8 @@
     map_ref,
     table_ref,
     load_sem,
+    out_ref,
+    out_sem,
     target,
     weights,
     send,
@@ -310,7 +312,7 @@
 
     sub128 = iota((128, 128), 0)
     lane128 = iota((128, 128), 1)
-    order = [2, 3, 1, 0]
+    order = [2, 3, 0, 1]
     arrival = [0, 1, 3, 2]
 
     def select_rows(first):
@@ -542,6 +544,8 @@
 
         surface = lax.fori_loop(0, blocks, backward, zero, unroll=True)
 
+    result = pltpu.make_async_copy(out_ref, out_hbm, out_sem)
+    result.start()
     region_part(surface, STEPS - 1)
 
     for mask in reversed(range(1, devices)):
@@ -558,6 +562,7 @@
     pltpu.make_async_copy(others, others, reg_recv).wait()
     reg_ref[...] = jnp.sum(part_in[...], axis=0)
 
+    result.wait()
     others = part.at[pl.ds(0, devices - 1)]
     pltpu.make_async_copy(others, others, reg_send).wait()
     for x in order:
@@ -608,7 +613,7 @@
             jax.ShapeDtypeStruct((STEPS, 128), F32),
         ),
         in_specs=[hbm] * 5 + [smem] + [hbm] * 5,
-        out_specs=(vmem, vmem),
+        out_specs=(hbm, vmem),
         scratch_shapes=[
             pltpu.VMEM((levels, per_device), F32),
             pltpu.VMEM((8, 128), F32),
@@ -621,6 +626,8 @@
             pltpu.VMEM((8, 128), I32),
             pltpu.VMEM((region_owner.shape[0] // 128, 128), I32),
             pltpu.SemaphoreType.DMA((10,)),
+            pltpu.VMEM(courant_x.shape, F32),
+            pltpu.SemaphoreType.DMA,
             pltpu.VMEM((8, 128), I32),
             pltpu.VMEM((2, 256, per_device), BF16),
             pltpu.VMEM((2, devices * 16, 128), F32),

time: 40.2 us -> 40 us (level)
  no operation moved by 1% of the time
where the time goes in v3:
time: 40 us; the launch traced here: 39.8 us
  Pallas kernels  36.3 us (91%)
  local copies, waits for them, and re-layouts  2.26 us (6%)
  between operations  1.3 us (3%)
    pallas_call x1, Pallas kernels, body(): pl.pallas_call(functools.partial(kernel, lat_count, devices), out_shape=(...  36.3 us
    unnamed x4, local copies, waits for them, and re-layouts  2.26 us

profile of v3, /device:TPU:0, one launch (start us, length us, event | category | flops | bytes accessed | tf_op | source)
XLA Modules:
  0.0 39.8 jit_solution(15090256731085914838)
XLA Ops:
  1.3 36.3 %shard_map.122 = (f32[72,8,128]{2,1,0:T(8,128)}, f32[2,128]{1,0:T(2,128)}) custom-call(f32[72,1024]{1,0:T(8,128)} %sk_hbm.1, f32[8,128]{1,0:T(8,128)} %bitcast.6, s32[8,128]{1,0:T(8,128)} %bitcast.7, s32[8,128]{1,0:T(8,128)} %bitcast.8, s32[8,128]{1,0:T(8,128)} %bitcast.9, s32[1]{0:T(128)S(6)} %copy.15.count_ref, f32[72,8,128]{2,1,0:T(8,128)} %cx_hbm.1, ...), custom_call_target="tpu_custom_call" | custom-call | tf_op jit(solution)/shard_map/pallas_call | solution.py:609
  37.5 0.0 copy-start
  37.6 1.7 %copy.16 = f32[72,8,128]{2,1,0:T(8,128)} copy(f32[72,8,128]{2,1,0:T(8,128)} %get-tuple-element.4) | data formatting | bytes 589824
  39.3 0.0 copy-done
  39.3 0.6 %copy.17 = f32[2,128]{1,0:T(2,128)} copy(f32[2,128]{1,0:T(2,128)S(1)} %copy-done) | data formatting | bytes 2048
Async XLA Ops:
  37.5 1.7 %copy-start = (f32[2,128]{1,0:T(2,128)S(1)}, f32[2,128]{1,0:T(2,128)}, u32[]{:S(2)}) copy-start(f32[2,128]{1,0:T(2,128)} %get-tuple-element.5) | copy-start | bytes 3076
